TPU v7x, 512 devices: a whole 4x8x8 slice. The times are simulated.
512 devices in a mesh: row: 16 (over y, core), col: 32 (over x, z).
Axes of the slice: x: 4, y: 8, z: 8, core: 2. Of those that a mesh axis runs over, the one named last changes fastest.
Arguments:
- matrix: float32 [16384, 16384], P('row', 'col'), may hold values from -4 to 4, as said below
- panel: float32 [16384, 64], P('row'), may hold values from -1200 to 1200
Outputs:
- updated: float32 [16384, 16384], P('row', 'col')
- w_rows: float32 [16384, 64], P('row')
- basis: float32 [16384, 64], P('row')
Inputs may be any that keep to these rules, and one draw needn't show every extreme that they name: Read in global order (both indices mapped back through their cyclic orders) the matrix is exactly symmetric.
All inputs are finite; a program needn't handle non-finite values.
Results may differ from a plain program's by a relative error of at most 0.00007.
Values sent between devices are 32-bit elements; how exact they have to be, the bound alone decides.
A program may use at most 64 MiB of HBM per device.

v0:
```python
import jax
import jax.numpy as jnp
from jax import lax
from jax.sharding import PartitionSpec as P

HIGH = lax.Precision.HIGHEST


def from_root(value, axis, source):
    kept = jnp.where(lax.axis_index(axis) == source, value, 0).astype(value.dtype)
    return lax.psum(kept, axis)


def matmul(left, right):
    return jnp.dot(left, right, precision=HIGH, preferred_element_type=jnp.float32)


def inner(left, right):
    return lax.dot_general(
        left, right, (((0,), (0,)), ((), ())), precision=HIGH, preferred_element_type=jnp.float32
    )


def pick_columns(values, cols_local):
    n_row = lax.axis_size("row")
    ratio = lax.axis_size("col") // n_row
    width = values.shape[1]
    blocks = values.reshape(cols_local // width, ratio, width, width)
    which = lax.axis_index("col") // n_row
    return lax.dynamic_index_in_dim(blocks, which, 1, keepdims=False).reshape(cols_local, width)


def local(matrix, panel):
    cols_local = matrix.shape[1]
    root = lax.axis_index("col") % lax.axis_size("row")
    gram = lax.psum(inner(panel, panel), "row")
    lower = lax.linalg.cholesky(gram)
    basis = lax.linalg.triangular_solve(lower, panel, left_side=False, lower=True, transpose_a=True)
    basis_cols = from_root(pick_columns(basis, cols_local), "row", root)
    partial_rows = matmul(matrix, basis_cols)
    product = lax.psum(partial_rows, "col")
    correction = lax.psum(inner(basis, product), "row")
    w_rows = 2.0 * (product - matmul(basis, correction))
    w_cols = from_root(pick_columns(w_rows, cols_local), "row", root)
    left = jnp.concatenate([basis, w_rows], axis=1)
    right = jnp.concatenate([w_cols, basis_cols], axis=1)
    updated = matrix - lax.dot_general(
        left, right, (((1,), (1,)), ((), ())), precision=HIGH, preferred_element_type=jnp.float32
    )
    return (updated, w_rows, basis)


def solution(mesh):
    return jax.shard_map(
        local,
        mesh=mesh,
        in_specs=(P("row", "col"), P("row", None)),
        out_specs=(P("row", "col"), P("row", None), P("row", None)),
        check_vma=False,
    )
```

profile of v0, /device:TPU:1, one launch (start us, length us, event | category | flops | bytes accessed | tf_op | source)
XLA Modules:
  0.0 520.1 jit_solution(12200631151645147567)
XLA Ops:
  7.2 0.0 copy-start
  7.2 0.0 copy-start.1
  7.2 0.0 all-reduce.4.cloned.1.call-start
  7.3 0.9 copy-done
  8.1 0.4 fusion.14
  8.5 49.0 %psum.35 = f32[64,64]{0,1:T(8,128)S(1)} all-reduce(f32[64,64]{0,1:T(8,128)S(1)} %fusion.14), channel_id=1, replica_groups=mesh['row'=16,'col'=32] {'row'}, use_global_device_ids=true, to_apply=%region_0.1 | all-reduce | flops 4096 | bytes 32768 | tf_op jit(solution)/shard_map/psum | solution.py:36
  57.5 0.1 copy.6
  57.6 5.8 %cholesky.16 = f32[64,64]{1,0:T(8,128)S(1)} custom-call(f32[64,64]{1,0:T(8,128)S(1)} %fusion.12), custom_call_target="Cholesky" | custom-call | tf_op jit(solution)/shard_map/cholesky | solution.py:37
  63.5 0.6 compare_reduce_fusion
  64.1 0.7 fusion.9
  64.8 4.9 custom-call.5
  69.7 0.4 fusion.10
  70.1 0.0 copy-start.2
  70.2 0.4 reshape.30
  70.6 0.8 fusion.4
  71.4 0.8 select_n.44
  72.2 0.0 all-reduce.4.cloned.1.call-update
  72.2 0.0 all-reduce.6.cloned.1.call-start
  72.3 115.0 %all-reduce.4.cloned.1.call-done = f32[512,64]{0,1:T(8,128)} async-done(((f32[512,64]{0,1:T(8,128)}), f32[512,64]{0,1:T(8,128)}) %all-reduce.4.cloned.1.call-update) | async-done | bytes 131088 | tf_op jit(solution)/shard_map/psum | solution.py:11
  187.2 0.0 copy-done.1
  187.2 3.7 convolution_bitcast_fusion
  191.0 0.0 copy-start.4
  191.0 0.0 all-reduce.6.cloned.1.call-update
  191.0 0.0 all-reduce.8.cloned.1.call-start
  191.0 152.5 %all-reduce.6.cloned.1.call-done = f32[1024,64]{0,1:T(8,128)} async-done(((f32[1024,64]{0,1:T(8,128)}), f32[1024,64]{0,1:T(8,128)}) %all-reduce.6.cloned.1.call-update) | async-done | bytes 262160 | tf_op jit(solution)/shard_map/psum | solution.py:41
  343.5 1.3 fusion.15
  344.8 47.2 %psum.38 = f32[64,64]{1,0:T(8,128)S(1)} all-reduce(f32[64,64]{1,0:T(8,128)S(1)} %fusion.15), channel_id=1, replica_groups=mesh['row'=16,'col'=32] {'row'}, use_global_device_ids=true, to_apply=%region_5.6 | all-reduce | flops 4096 | bytes 32768 | tf_op jit(solution)/shard_map/psum | solution.py:42
  392.1 1.4 fusion
  393.4 0.0 copy-start.3
  393.5 0.4 reshape.31
  393.8 1.5 fusion.5
  395.4 1.7 select_n.46
  397.1 0.0 all-reduce.8.cloned.1.call-update
  397.1 112.4 %all-reduce.8.cloned.1.call-done = f32[512,64]{0,1:T(8,128)} async-done(((f32[512,64]{0,1:T(8,128)}), f32[512,64]{0,1:T(8,128)}) %all-reduce.8.cloned.1.call-update) | async-done | bytes 131088 | tf_op jit(solution)/shard_map/psum | solution.py:11
  509.5 0.0 copy-done.2
  509.5 0.0 copy-done.4
  509.5 4.1 convolution_subtract_fusion
  513.6 0.0 copy-done.3
  (2 shorter events, 0.0 us)
Async XLA Ops:
  7.2 1.0 copy-start
  7.2 180.1 %copy-start.1 = (f32[1024,512]{1,0:T(8,128)S(1)}, f32[1024,512]{1,0:T(8,128)}, u32[]{:S(2)}) copy-start(f32[1024,512]{1,0:T(8,128)} %param.2) | copy-start | bytes 6291460
  7.2 180.0 %all-reduce.4.cloned.1.call-start = ((), (), s32[]{:S(2)}) async-start(), calls=%async_computation | async-start | bytes 262144 | tf_op jit(solution)/shard_map/psum | solution.py:11
  70.1 439.3 %copy-start.2 = (f32[64,1024]{1,0:T(8,128)}, f32[64,1024]{1,0:T(8,128)S(1)}, u32[]{:S(2)}) copy-start(f32[64,1024]{1,0:T(8,128)S(1)} %fusion.10) | copy-start | bytes 786436
  72.2 271.3 %all-reduce.6.cloned.1.call-start = ((), (), s32[]{:S(2)}) async-start(), calls=%async_computation.1 | async-start | bytes 524288 | tf_op jit(solution)/shard_map/psum | solution.py:41
  191.0 318.5 %copy-start.4 = (f32[512,64]{0,1:T(8,128)S(1)}, f32[512,64]{0,1:T(8,128)}, u32[]{:S(2)}) copy-start(f32[512,64]{0,1:T(8,128)} %all-reduce.4.cloned.1.call-done) | copy-start | bytes 393220
  191.0 318.5 %all-reduce.8.cloned.1.call-start = ((), (), s32[]{:S(2)}) async-start(), calls=%async_computation.2 | async-start | bytes 262144 | tf_op jit(solution)/shard_map/psum | solution.py:11
  393.4 120.1 %copy-start.3 = (f32[1024,64]{0,1:T(8,128)}, f32[1024,64]{0,1:T(8,128)S(1)}, u32[]{:S(2)}) copy-start(f32[1024,64]{0,1:T(8,128)S(1)} %fusion) | copy-start | bytes 786436
Sparse Core Ops, SparseCore 0:
  72.3 114.8 all-reduce.3
  191.6 151.8 all-reduce.5
  397.2 112.1 all-reduce.7
where the time goes:
time: 520 us
  waiting for transfers between devices  380 us (73%)
  blocking collectives  96.3 us (19%)
  other arithmetic  14.5 us (3%)
  between operations  13.9 us (3%)
  matrix products  11.3 us (2%)
    psum x2, waiting for transfers between devices, from_root(): return lax.psum(kept, axis)  227 us
    psum x1, waiting for transfers between devices, local(): product = lax.psum(partial_rows, 'col')  152 us
    psum x1, blocking collectives, local(): gram = lax.psum(inner(panel, panel), 'row')  49 us
    psum x1, blocking collectives, local(): correction = lax.psum(inner(basis, product), 'row')  47.2 us
  transfers between devices with their start and end apart: 3, of which 3 were waited for; matrix products, arithmetic and copies ran while one was open for 0% of the time, Pallas kernels for 0%

commit v1 on v0

v1 whole, which is shorter than its diff:
```python
import functools

import jax
import jax.numpy as jnp
from jax import lax
from jax.experimental import pallas as pl
from jax.experimental.pallas import tpu as pltpu
from jax.sharding import PartitionSpec as P

MESH = pl.DeviceIdType.MESH
HIGH = lax.Precision.HIGHEST
F32 = jnp.float32


def dot(left, right, dims=((1,), (0,))):
    return lax.dot_general(left, right, (dims, ((), ())), precision=HIGH, preferred_element_type=F32)


def whole(ref, lead):
    rows = []
    for y in range(8):
        rows.append(jnp.concatenate([ref[lead + (2 * y,)], ref[lead + (2 * y + 1,)]], axis=1))
    return jnp.concatenate(rows, axis=0)


def eliminate(aug, first, last):
    ids = lax.broadcasted_iota(jnp.int32, (64, 1), 0)
    for j in range(first, last):
        row = aug[j : j + 1, :]
        factor = aug[:, j : j + 1] * (1.0 / row[:, j : j + 1])
        aug = aug - jnp.where(ids > j, factor, 0.0) * row
    return aug


def exchange(
    mat, pan, v_out, w_out, right_out,
    gsend, grecv, psend, precv, xsend, xrecv, piece, acol, arow, tsend, trecv, usend, urecv,
    ssem, rsem,
):
    r, c = lax.axis_index("row"), lax.axis_index("col")
    y, core, x, z = r // 2, r % 2, c // 8, c % 8
    half, root = c // 16, c % 16

    def put(src, dst, k, row, col):
        pltpu.make_async_remote_copy(
            src_ref=src, dst_ref=dst, send_sem=ssem.at[k], recv_sem=rsem.at[k],
            device_id={"row": row, "col": col}, device_id_type=MESH,
        ).start()

    def keep(src, dst, k):
        pltpu.make_async_copy(src, dst, rsem.at[k]).start()

    def got(ref, k):
        pltpu.make_async_copy(ref, ref, rsem.at[k]).wait()

    def sent(ref, k):
        pltpu.make_async_copy(ref, ref, ssem.at[k]).wait()

    def loop(first, last, body):
        lax.fori_loop(first, last, lambda i, s: (body(i), s)[1], 0)

    mine = jnp.concatenate(
        [pan[pl.ds(pl.multiple_of(128 * k + 64 * half, 64), 64), :] for k in range(8)], axis=0
    )
    psend[...] = mine.T

    @pl.when(root == r)
    def _():
        keep(psend, precv, 0)

    @pl.when(root != r)
    def _():
        put(psend, precv, 0, root, r + 16 * half)

    pant = pan[...].T
    gram = dot(pant, pan[...])
    gsend[...] = jnp.concatenate([gram[:32], gram[32:]], axis=1)
    keep(gsend, grecv.at[r], 1)
    loop(1, 16, lambda i: put(gsend, grecv.at[r], 1, (r + i) % 16, c))

    prod = dot(pant, mat[...])
    for k in range(16):
        xsend[k] = prod[8 * (k // 2) : 8 * (k // 2) + 8, 256 * (k % 2) : 256 * (k % 2) + 256]
    keep(xsend.at[r], xrecv.at[r], 2)

    def scatter(i):
        d = (r + i) % 16
        put(xsend.at[d], xrecv.at[r], 2, d, c)

    loop(1, 16, scatter)
    got(xrecv, 2)
    total = xrecv[0]
    for k in range(1, 16):
        total = total + xrecv[k]
    piece[...] = total

    got(precv, 0)
    tpart = dot(total, precv[:, pl.ds(pl.multiple_of(256 * core, 256), 256)], ((1,), (1,)))
    tsend[...] = jnp.concatenate([tpart, tpart], axis=1)
    me = z * 2 + core
    keep(tsend, trecv.at[me], 3)

    def share(i):
        d = (me + i) % 16
        put(tsend, trecv.at[me], 3, y * 2 + d % 2, x * 8 + d // 2)

    loop(1, 16, share)

    loop(1, 32, lambda i: put(piece, arow.at[half, r], 4, root, (c + i) % 32))

    @pl.when(root == r)
    def _():
        keep(piece, arow.at[half, r], 4)

    @pl.when(root != r)
    def _():
        put(piece, arow.at[half, r], 4, root, c)

    keep(piece, acol.at[r], 5)
    loop(1, 16, lambda i: put(piece, acol.at[r], 5, (r + i) % 16, c))

    got(grecv, 1)
    packed = grecv[0]
    for k in range(1, 16):
        packed = packed + grecv[k]
    gram = jnp.concatenate([packed[:, :64], packed[:, 64:]], axis=0)
    eye = (
        lax.broadcasted_iota(jnp.int32, (64, 64), 0) == lax.broadcasted_iota(jnp.int32, (64, 64), 1)
    ).astype(F32)
    aug = eliminate(jnp.concatenate([gram, eye], axis=1), 0, 24)

    got(trecv, 3)
    total = trecv[0]
    for k in range(1, 16):
        total = total + trecv[k]
    usend[...] = total
    place = x * 8 + y
    keep(usend, urecv.at[place], 6)

    def share2(i):
        d = (place + i) % 32
        put(usend, urecv.at[place], 6, (d % 8) * 2 + core, (d // 8) * 8 + z)

    loop(1, 32, share2)

    aug = eliminate(aug, 24, 64)
    diag = jnp.sum(aug[:, :64] * eye, axis=1, keepdims=True)
    linv = aug[:, 64:] * lax.rsqrt(diag)

    v_rows = dot(pan[...], linv, ((1,), (1,)))
    v_out[...] = v_rows
    v_cols = dot(linv, precv[...])

    got(acol, 5)
    av_cols = dot(linv, whole(acol, ()))
    got(arow, 4)
    av_rows = [dot(linv, whole(arow, (h,))).T for h in range(2)]
    av_rows = jnp.concatenate(
        [av_rows[h][64 * k : 64 * k + 64] for k in range(8) for h in range(2)], axis=0
    )

    got(urecv, 6)
    rows = []
    for k in range(8):
        rows.append(urecv[k] + urecv[8 + k] + urecv[16 + k] + urecv[24 + k])
    corr = 2.0 * dot(dot(linv, jnp.concatenate(rows, axis=0)[:, :64]), linv, ((1,), (1,)))
    w_out[...] = 2.0 * av_rows - dot(v_rows, corr)
    right_out[:64] = 2.0 * av_cols - dot(corr, v_cols, ((0,), (0,)))
    right_out[64:] = v_cols

    @pl.when(root != r)
    def _():
        sent(psend, 0)
        sent(arow, 4)

    @pl.when(root == r)
    def _():
        sent(arow.at[0], 4)
        sent(arow.at[1, pl.ds(0, 15)], 4)

    sent(grecv.at[pl.ds(0, 15)], 1)
    sent(xrecv.at[pl.ds(0, 15)], 2)
    sent(trecv.at[pl.ds(0, 15)], 3)
    sent(acol.at[pl.ds(0, 15)], 5)
    sent(urecv.at[pl.ds(0, 31)], 6)


def update(mat, v_rows, w_rows, right, out, w_out, v_out):
    left = jnp.concatenate([v_rows[...], w_rows[...]], axis=1)
    out[...] = mat[...] - dot(left, right[...])
    w_out[...] = w_rows[...]
    v_out[...] = v_rows[...]


def local(mat, pan):
    vmem = pl.BlockSpec(memory_space=pltpu.VMEM)
    v_rows, w_rows, right = pl.pallas_call(
        exchange,
        out_shape=[
            jax.ShapeDtypeStruct((1024, 64), F32),
            jax.ShapeDtypeStruct((1024, 64), F32),
            jax.ShapeDtypeStruct((128, 512), F32),
        ],
        in_specs=[vmem, vmem],
        out_specs=[vmem] * 3,
        scratch_shapes=[
            pltpu.VMEM((32, 128), F32),
            pltpu.VMEM((16, 32, 128), F32),
            pltpu.VMEM((64, 512), F32),
            pltpu.VMEM((64, 512), F32),
            pltpu.VMEM((16, 8, 256), F32),
            pltpu.VMEM((16, 8, 256), F32),
            pltpu.VMEM((8, 256), F32),
            pltpu.VMEM((16, 8, 256), F32),
            pltpu.VMEM((2, 16, 8, 256), F32),
            pltpu.VMEM((8, 128), F32),
            pltpu.VMEM((16, 8, 128), F32),
            pltpu.VMEM((8, 128), F32),
            pltpu.VMEM((32, 8, 128), F32),
            pltpu.SemaphoreType.DMA((7,)),
            pltpu.SemaphoreType.DMA((7,)),
        ],
        compiler_params=pltpu.CompilerParams(has_side_effects=True, vmem_limit_bytes=48 * 1024 * 1024),
    )(mat, pan)
    steps, rows = 8, 128
    by_row = lambda width: pl.BlockSpec((rows, width), lambda i: (i, 0))
    return pl.pallas_call(
        update,
        grid=(steps,),
        out_shape=[
            jax.ShapeDtypeStruct((1024, 512), F32),
            jax.ShapeDtypeStruct((1024, 64), F32),
            jax.ShapeDtypeStruct((1024, 64), F32),
        ],
        in_specs=[by_row(512), by_row(64), by_row(64), pl.BlockSpec((128, 512), lambda i: (0, 0))],
        out_specs=[by_row(512), by_row(64), by_row(64)],
        compiler_params=pltpu.CompilerParams(vmem_limit_bytes=32 * 1024 * 1024),
    )(mat, v_rows, w_rows, right)


def solution(mesh):
    return jax.shard_map(
        local,
        mesh=mesh,
        in_specs=(P("row", "col"), P("row", None)),
        out_specs=(P("row", "col"), P("row", None), P("row", None)),
        check_vma=False,
    )
```

time: 520 us -> 98.8 us (0.19)
  waiting for transfers between devices: 380 us -> 0 us
  blocking collectives: 96.3 us -> 0 us
  Pallas kernels: 0 us -> 93.5 us
  other arithmetic: 14.5 us -> 0 us
  between operations: 13.9 us -> 0.66 us
  matrix products: 11.3 us -> 0 us
    psum x3 -> x0, waiting for transfers between devices: 380 us -> none  [the longest x2 227 us: from_root(): return lax.psum(kept, axis)]
    psum x2 -> x0, blocking collectives: 96.3 us -> none  [the longest x1 49 us: local(): gram = lax.psum(inner(panel, panel), 'row')]
    pallas_call x0 -> x2, Pallas kernels: none -> 93.5 us  [the longest x1 88.5 us: local(): pl.pallas_call(exchange, out_shape=[jax.ShapeDtypeStruct((1024, 64), F32)...]
    another operation x5 -> x0, other arithmetic: 12.1 us -> none  [the longest x3 6.52 us: local(): lower = lax.linalg.cholesky(gram)]
    dot_general x5 -> x0, matrix products: 10.8 us -> none  [the longest x2 5.1 us: matmul(): jnp.dot(left, right, precision=HIGH, preferred_element_type=jnp.float32)]
  transfers between devices with their start and end apart: 3 -> 0, of which waited for: 3 -> 0; matrix products, arithmetic and copies ran while one was open for 0% -> 0% of each run, Pallas kernels for 0% -> 0%
where the time goes in v1:
time: 98.8 us; the launch traced here: 98.7 us
  Pallas kernels  93.5 us (95%)
  local copies, waits for them, and re-layouts  4.51 us (5%)
    pallas_call x1, Pallas kernels, local(): pl.pallas_call(exchange, out_shape=[jax.ShapeDtypeStruct((1024, 64), F32)...  88.5 us
    pallas_call x1, Pallas kernels, local(): pl.pallas_call(update, grid=(steps,), out_shape=[jax.ShapeDtypeStruct((10...  4.95 us
    unnamed x3, local copies, waits for them, and re-layouts  2.73 us

profile of v1, /device:TPU:1, one launch (start us, length us, event | category | flops | bytes accessed | tf_op | source)
XLA Modules:
  0.0 98.7 jit_solution(9082224615274757310)
XLA Ops:
  0.6 1.1 %copy.5.pan = f32[1024,64]{1,0:T(8,128)S(1)} copy(f32[1024,64]{0,1:T(8,128)} %param.3) | data formatting | bytes 524288 | tf_op args[1]
  1.8 0.0 copy-start
  1.8 1.6 %copy-done = f32[1024,512]{1,0:T(8,128)S(1)} copy-done((f32[1024,512]{1,0:T(8,128)S(1)}, f32[1024,512]{1,0:T(8,128)}, u32[]{:S(2)}) %copy-start) | copy-done | bytes 2097176
  3.4 88.5 %shard_map.49 = (f32[1024,64]{1,0:T(8,128)S(1)}, f32[1024,64]{1,0:T(8,128)S(1)}, f32[128,512]{1,0:T(8,128)S(1)}) custom-call(f32[1024,512]{1,0:T(8,128)S(1)} %copy-done, f32[1024,64]{1,0:T(8,128)S(1)} %copy.5.pan), custom_call_target="tpu_custom_call" | custom-call | tf_op jit(solution)/shard_map/pallas_call | solution.py:197
  91.9 5.0 %shard_map.50 = (f32[1024,512]{1,0:T(8,128)}, f32[1024,64]{1,0:T(8,128)S(1)}, f32[1024,64]{1,0:T(8,128)S(1)}) custom-call(f32[1024,512]{1,0:T(8,128)S(1)} %copy-done, f32[1024,64]{1,0:T(8,128)S(1)} %get-tuple-element.6.v_rows, f32[1024,64]{1,0:T(8,128)S(1)} %get-tuple-element.7.w_rows, f32[128,512]{1,0:T(8,128)S(1)} %get-tuple-element.8.right), custom_call_target="tpu_custom_call" | custom-call | tf_op jit(solution)/shard_map/pallas_call | solution.py:227
  96.9 0.9 copy.6
  97.8 0.9 copy.7
Async XLA Ops:
  1.8 1.6 %copy-start = (f32[1024,512]{1,0:T(8,128)S(1)}, f32[1024,512]{1,0:T(8,128)}, u32[]{:S(2)}) copy-start(f32[1024,512]{1,0:T(8,128)} %mat.3) | copy-start | bytes 6291460

commit v2 on v0

v2 whole, which is shorter than its diff:
```python
import jax
import jax.numpy as jnp
from jax import lax
from jax.experimental import pallas as pl
from jax.experimental.pallas import tpu as pltpu
from jax.sharding import PartitionSpec as P

VLIM = 40
SPACE = pltpu.HBM
CUT1 = 0
CUT2 = 24
ROWS = 256
MESH = pl.DeviceIdType.MESH
HIGH = lax.Precision.HIGHEST
F32 = jnp.float32
BF16 = jnp.bfloat16


def dot(left, right, dims=((1,), (0,))):
    return lax.dot_general(left, right, (dims, ((), ())), precision=HIGH, preferred_element_type=F32)


def split(value):
    high = value.astype(BF16)
    return high, (value - high.astype(F32)).astype(BF16)


def whole(ref, lead):
    rows = []
    for y in range(8):
        rows.append(jnp.concatenate([ref[lead + (2 * y,)], ref[lead + (2 * y + 1,)]], axis=1))
    return jnp.concatenate(rows, axis=0)


def eliminate(aug, first, last):
    ids = lax.broadcasted_iota(jnp.int32, (64, 1), 0)
    for j in range(first, last):
        row = aug[j : j + 1, :]
        factor = aug[:, j : j + 1] * (1.0 / row[:, j : j + 1])
        aug = aug - jnp.where(ids > j, factor, 0.0) * row
    return aug


def exchange(
    mat_hbm, pan_hbm, out,
    mat, pan, gsend, grecv, qsend, gall, psend, precv, xsend, xrecv, piece, moved, acol, arow,
    tsend, trecv, usend, urecv,
    ssem, rsem, msem,
):
    r, c = lax.axis_index("row"), lax.axis_index("col")
    y, core, x, z = r // 2, r % 2, c // 8, c % 8
    drains = []

    def put(src, dst, k, row, col, recv=None):
        pltpu.make_async_remote_copy(
            src_ref=src, dst_ref=dst, send_sem=ssem.at[k], recv_sem=rsem.at[k if recv is None else recv],
            device_id={"row": row, "col": col}, device_id_type=MESH,
        ).start()

    def keep(src, dst, k):
        pltpu.make_async_copy(src, dst, rsem.at[k]).start()

    def got(ref, k):
        pltpu.make_async_copy(ref, ref, rsem.at[k]).wait()

    def sent(ref, k):
        drains.append(lambda: pltpu.make_async_copy(ref, ref, ssem.at[k]).wait())

    def loop(first, last, body):
        lax.fori_loop(first, last, lambda i, s: (body(i), s)[1], 0)

    def finish():
        for drain in drains:
            drain()

    barrier = pltpu.get_barrier_semaphore()

    def greet(row, col):
        pl.semaphore_signal(barrier, inc=1, device_id={"row": row, "col": col}, device_id_type=MESH)

    load = pltpu.make_async_copy(mat_hbm, mat, msem.at[0])
    load.start()
    load_pan = pltpu.make_async_copy(pan_hbm, pan, msem.at[1])
    load_pan.start()

    core_to = (x - r // 8) % 2
    x_to = (x - core_to) % 4
    y_to = (z - r % 8 + y + 4) % 8
    half_to = x_to // 2
    row_to, col_to = 2 * y_to + core_to, 8 * x_to + r % 8
    row_up, col_up = c % 16, 8 * ((x + core) % 4) + (z + y - (c % 16) // 2 + 4) % 8
    greet(row_to, col_to)
    greet(row_up, col_up)
    loop(1, 16, lambda i: greet((r + i) % 16, c))
    loop(1, 8, lambda i: greet(r, 8 * x + (z + i) % 8))
    loop(1, 4, lambda i: greet(r, 8 * ((x + i) % 4) + z))

    load_pan.wait()
    for k in range(4):
        low, high = pan[:, 256 * k : 256 * k + 128], pan[:, 256 * k + 128 : 256 * k + 256]
        psend[k // 2, :, 128 * (k % 2) : 128 * (k % 2) + 128] = jnp.where(
            half_to == 0,
            jnp.concatenate([low[:, :64], high[:, :64]], axis=1),
            jnp.concatenate([low[:, 64:], high[:, 64:]], axis=1),
        )
    pant = pan[...]
    gram = dot(pant, pant, ((1,), (1,)))
    gsend[...] = jnp.concatenate([gram[:32], gram[32:]], axis=1)
    load.wait()
    ph, pl_ = split(pant)
    ah, al = split(mat[...])
    both = jnp.dot(jnp.concatenate([ph, pl_], axis=0), ah, preferred_element_type=F32)
    prod = both[:64] + (both[64:] + jnp.dot(ph, al, preferred_element_type=F32))
    for k in range(16):
        xsend[k] = prod[8 * (k // 2) : 8 * (k // 2) + 8, 256 * (k % 2) : 256 * (k % 2) + 256]

    pl.semaphore_wait(barrier, 27)
    put(psend.at[core_to], precv.at[core_to], 0, row_to, col_to)

    def scatter(i):
        d = (r + 8 + i) % 16

        @pl.when(i != 8)
        def _():
            put(xsend.at[d], xrecv.at[r], 3, d, c)

    loop(0, 16, scatter)
    keep(xsend.at[r], xrecv.at[r], 3)
    share = gsend.at[pl.ds(pl.multiple_of(8 * x, 8), 8)]
    loop(1, 16, lambda i: put(share, grecv.at[r], 2, (r + i) % 16, c))
    keep(share, grecv.at[r], 2)
    put(psend.at[1 - core_to], precv.at[1 - core_to], 1, row_to, col_to)
    sent(psend.at[0], 0)
    sent(xrecv.at[pl.ds(0, 15)], 3)
    sent(grecv.at[pl.ds(0, 15)], 2)
    sent(psend.at[0], 1)
    got(xrecv, 3)
    total = xrecv[0]
    for k in range(1, 16):
        total = total + xrecv[k]
    piece[...] = total
    put(piece, moved, 4, row_up, col_up)
    sent(piece, 4)

    got(precv.at[core], 0)
    tpart = dot(total, precv[core], ((1,), (1,)))
    tsend[...] = jnp.concatenate([tpart[:4], tpart[4:]], axis=1)
    me = 2 * z + core

    def share_z(i):
        d = (me + i) % 16
        put(tsend, trecv.at[me], 5, 2 * y + d % 2, 8 * x + d // 2)

    loop(1, 16, share_z)
    keep(tsend, trecv.at[me], 5)
    sent(trecv.at[pl.ds(0, 15)], 5)

    got(grecv, 2)
    quarter = grecv[0]
    for k in range(1, 16):
        quarter = quarter + grecv[k]
    qsend[...] = quarter
    loop(1, 4, lambda i: put(qsend, gall.at[x], 8, r, 8 * ((x + i) % 4) + z))
    keep(qsend, gall.at[x], 8)
    sent(gall.at[pl.ds(0, 3)], 8)

    loop(1, 16, lambda i: put(piece, acol.at[r], 6, (r + i) % 16, c))
    keep(piece, acol.at[r], 6)
    sent(acol.at[pl.ds(0, 15)], 6)

    got(gall, 8)
    packed = jnp.concatenate([gall[k] for k in range(4)], axis=0)
    gram = jnp.concatenate([packed[:, :64], packed[:, 64:]], axis=0)
    eye = (
        lax.broadcasted_iota(jnp.int32, (64, 64), 0) == lax.broadcasted_iota(jnp.int32, (64, 64), 1)
    ).astype(F32)
    aug = jnp.concatenate([gram, eye], axis=1)
    aug = eliminate(aug, 0, CUT1)

    got(moved, 4)
    loop(1, 32, lambda i: put(moved, arow.at[half_to, row_to], 9, r, (c + i) % 32))
    keep(moved, arow.at[half_to, row_to], 9)
    sent(arow.at[0, pl.ds(0, 15)], 9)
    sent(arow.at[1], 9)

    aug = eliminate(aug, CUT1, CUT2)
    got(trecv, 5)
    total = trecv[0]
    for k in range(1, 16):
        total = total + trecv[k]
    usend[...] = total
    place = 8 * x + y

    def share_xy(i):
        d = (place + i) % 32
        put(usend, urecv.at[place], 7, 2 * (d % 8) + core, 8 * (d // 8) + z)

    loop(1, 32, share_xy)
    keep(usend, urecv.at[place], 7)
    sent(urecv.at[pl.ds(0, 31)], 7)
    aug = eliminate(aug, CUT2, 64)
    diag = jnp.sum(aug[:, :64] * eye, axis=1, keepdims=True)
    linv = aug[:, 64:] * lax.rsqrt(diag)

    v_rows = dot(linv, pant)
    out[:, :1024] = v_rows
    got(precv.at[0], 1)
    v_cols = dot(linv, jnp.concatenate([precv[0], precv[1]], axis=1))
    out[:, 2048:2560] = v_cols
    got(acol, 6)
    av_cols = dot(linv, whole(acol, ()))

    got(arow, 9)
    even, odd = whole(arow, (0,)), whole(arow, (1,))
    blocks = []
    for k in range(8):
        blocks += [even[:, 64 * k : 64 * k + 64], odd[:, 64 * k : 64 * k + 64]]
    av_rows = dot(linv, jnp.concatenate(blocks, axis=1))

    got(urecv, 7)
    rows = []
    for k in range(8):
        pair = (urecv[k] + urecv[8 + k]) + (urecv[16 + k] + urecv[24 + k])
        rows += [pair[:, :64], pair[:, 64:]]
    corr = 2.0 * dot(dot(linv, jnp.concatenate(rows, axis=0)), linv, ((1,), (1,)))
    out[:, 1024:2048] = 2.0 * av_rows - dot(corr, v_rows, ((0,), (0,)))
    out[:, 2560:] = 2.0 * av_cols - dot(corr, v_cols, ((0,), (0,)))
    finish()


def update(mat, parts, out, w_out, v_out):
    step = pl.program_id(0)
    first = pl.multiple_of(ROWS * step, ROWS)
    v_rows, w_rows = parts[:, pl.ds(first, ROWS)], parts[:, pl.ds(1024 + first, ROWS)]
    lh, ll = split(jnp.concatenate([v_rows, w_rows], axis=0).T)
    rh, rl = split(jnp.concatenate([parts[:, 2560:], parts[:, 2048:2560]], axis=0))
    out[...] = mat[...] - jnp.dot(
        jnp.concatenate([lh, lh, ll], axis=1), jnp.concatenate([rh, rl, rh], axis=0),
        preferred_element_type=F32,
    )
    w_out[...] = w_rows
    v_out[...] = v_rows


def local(mat, pan):
    vmem = pl.BlockSpec(memory_space=pltpu.VMEM)
    parts = pl.pallas_call(
        exchange,
        out_shape=jax.ShapeDtypeStruct((64, 3072), F32),
        in_specs=[pl.BlockSpec(memory_space=SPACE)] * 2,
        out_specs=vmem,
        scratch_shapes=[
            pltpu.VMEM((1024, 512), F32),
            pltpu.VMEM((64, 1024), F32),
            pltpu.VMEM((32, 128), F32),
            pltpu.VMEM((16, 8, 128), F32),
            pltpu.VMEM((8, 128), F32),
            pltpu.VMEM((4, 8, 128), F32),
            pltpu.VMEM((2, 64, 256), F32),
            pltpu.VMEM((2, 64, 256), F32),
            pltpu.VMEM((16, 8, 256), F32),
            pltpu.VMEM((16, 8, 256), F32),
            pltpu.VMEM((8, 256), F32),
            pltpu.VMEM((8, 256), F32),
            pltpu.VMEM((16, 8, 256), F32),
            pltpu.VMEM((2, 16, 8, 256), F32),
            pltpu.VMEM((4, 128), F32),
            pltpu.VMEM((16, 4, 128), F32),
            pltpu.VMEM((4, 128), F32),
            pltpu.VMEM((32, 4, 128), F32),
            pltpu.SemaphoreType.DMA((10,)),
            pltpu.SemaphoreType.DMA((10,)),
            pltpu.SemaphoreType.DMA((2,)),
        ],
        compiler_params=pltpu.CompilerParams(
            has_side_effects=True, collective_id=0, vmem_limit_bytes=VLIM * 1024 * 1024
        ),
    )(mat, pan.T)
    across = pl.BlockSpec((64, ROWS), lambda i: (0, i))
    down = pl.BlockSpec((ROWS, 512), lambda i: (i, 0))
    updated, w_rows, v_rows = pl.pallas_call(
        update,
        grid=(1024 // ROWS,),
        out_shape=[
            jax.ShapeDtypeStruct((1024, 512), F32),
            jax.ShapeDtypeStruct((64, 1024), F32),
            jax.ShapeDtypeStruct((64, 1024), F32),
        ],
        in_specs=[down, pl.BlockSpec((64, 3072), lambda i: (0, 0))],
        out_specs=[down, across, across],
        compiler_params=pltpu.CompilerParams(vmem_limit_bytes=32 * 1024 * 1024),
    )(mat, parts)
    return updated, w_rows.T, v_rows.T


def solution(mesh):
    return jax.shard_map(
        local,
        mesh=mesh,
        in_specs=(P("row", "col"), P("row", None)),
        out_specs=(P("row", "col"), P("row", None), P("row", None)),
        check_vma=False,
    )
```

time: 520 us -> 46.4 us (0.09)
  waiting for transfers between devices: 380 us -> 0 us
  blocking collectives: 96.3 us -> 0 us
  Pallas kernels: 0 us -> 43.1 us
  other arithmetic: 14.5 us -> 0 us
  between operations: 13.9 us -> 0.65 us
  matrix products: 11.3 us -> 0 us
    psum x3 -> x0, waiting for transfers between devices: 380 us -> none  [the longest x2 227 us: from_root(): return lax.psum(kept, axis)]
    psum x2 -> x0, blocking collectives: 96.3 us -> none  [the longest x1 49 us: local(): gram = lax.psum(inner(panel, panel), 'row')]
    pallas_call x0 -> x2, Pallas kernels: none -> 43.1 us  [the longest x1 40.4 us: local(): pl.pallas_call(exchange, out_shape=jax.ShapeDtypeStruct((64, 3072), F32),...]
    another operation x5 -> x0, other arithmetic: 12.1 us -> none  [the longest x3 6.52 us: local(): lower = lax.linalg.cholesky(gram)]
    dot_general x5 -> x0, matrix products: 10.8 us -> none  [the longest x2 5.1 us: matmul(): jnp.dot(left, right, precision=HIGH, preferred_element_type=jnp.float32)]
  transfers between devices with their start and end apart: 3 -> 0, of which waited for: 3 -> 0; matrix products, arithmetic and copies ran while one was open for 0% -> 0% of each run, Pallas kernels for 0% -> 0%
where the time goes in v2:
time: 46.4 us; the launch traced here: 46.2 us
  Pallas kernels  43.1 us (93%)
  local copies, waits for them, and re-layouts  2.53 us (5%)
  between operations  0.65 us (1%)
    pallas_call x1, Pallas kernels, local(): pl.pallas_call(exchange, out_shape=jax.ShapeDtypeStruct((64, 3072), F32),...  40.4 us
    pallas_call x1, Pallas kernels, local(): pl.pallas_call(update, grid=(1024 // ROWS,), out_shape=[jax.ShapeDtypeStr...  2.69 us
    unnamed x4, local copies, waits for them, and re-layouts  2.53 us

profile of v2, /device:TPU:1, one launch (start us, length us, event | category | flops | bytes accessed | tf_op | source)
XLA Modules:
  0.0 46.2 jit_solution(1615432816168934059)
XLA Ops:
  0.6 0.0 copy-start
  0.6 1.6 %copy-done = f32[1024,512]{1,0:T(8,128)S(1)} copy-done((f32[1024,512]{1,0:T(8,128)S(1)}, f32[1024,512]{1,0:T(8,128)}, u32[]{:S(2)}) %copy-start) | copy-done | bytes 2097176
  2.2 0.0 copy-start.1
  2.2 0.9 %copy-done.1 = f32[1024,64]{0,1:T(8,128)S(1)} copy-done((f32[1024,64]{0,1:T(8,128)S(1)}, f32[1024,64]{0,1:T(8,128)}, u32[]{:S(2)}) %copy-start.1) | copy-done | bytes 262168
  3.2 40.4 %shard_map.49.parts = f32[64,3072]{1,0:T(8,128)S(1)} custom-call(f32[1024,512]{1,0:T(8,128)S(1)} %copy-done, f32[64,1024]{1,0:T(8,128)S(1)} %bitcast.3), custom_call_target="tpu_custom_call" | custom-call | tf_op jit(solution)/shard_map/pallas_call | solution.py:247
  43.5 2.7 %shard_map.50 = (f32[1024,512]{1,0:T(8,128)}, f32[64,1024]{1,0:T(8,128)}, f32[64,1024]{1,0:T(8,128)}) custom-call(f32[1024,512]{1,0:T(8,128)S(1)} %copy-done, f32[64,3072]{1,0:T(8,128)S(1)} %shard_map.49.parts), custom_call_target="tpu_custom_call" | custom-call | tf_op jit(solution)/shard_map/pallas_call | solution.py:281
Async XLA Ops:
  0.6 1.6 %copy-start = (f32[1024,512]{1,0:T(8,128)S(1)}, f32[1024,512]{1,0:T(8,128)}, u32[]{:S(2)}) copy-start(f32[1024,512]{1,0:T(8,128)} %mat.1) | copy-start | bytes 6291460
  2.2 0.9 %copy-start.1 = (f32[1024,64]{0,1:T(8,128)S(1)}, f32[1024,64]{0,1:T(8,128)}, u32[]{:S(2)}) copy-start(f32[1024,64]{0,1:T(8,128)} %param.3) | copy-start | bytes 786436

commit v3 on v2

--- a/solution.py
+++ b/solution.py
@@ -5,11 +5,6 @@
 from jax.experimental.pallas import tpu as pltpu
 from jax.sharding import PartitionSpec as P
 
-VLIM = 40
-SPACE = pltpu.HBM
-CUT1 = 0
-CUT2 = 24
-ROWS = 256
 MESH = pl.DeviceIdType.MESH
 HIGH = lax.Precision.HIGHEST
 F32 = jnp.float32
@@ -25,27 +20,43 @@
     return high, (value - high.astype(F32)).astype(BF16)
 
 
-def whole(ref, lead):
-    rows = []
-    for y in range(8):
-        rows.append(jnp.concatenate([ref[lead + (2 * y,)], ref[lead + (2 * y + 1,)]], axis=1))
-    return jnp.concatenate(rows, axis=0)
-
-
-def eliminate(aug, first, last):
-    ids = lax.broadcasted_iota(jnp.int32, (64, 1), 0)
-    for j in range(first, last):
+def dot3(left, right, dims=((1,), (0,))):
+    lh, ll = split(left)
+    rh, rl = split(right)
+
+    def one(u, v):
+        return lax.dot_general(u, v, (dims, ((), ())), preferred_element_type=F32)
+
+    return one(lh, rh) + (one(lh, rl) + one(ll, rh))
+
+
+def whole(piece):
+    return jnp.concatenate(
+        [jnp.concatenate([piece(y, 0), piece(y, 1)], axis=1) for y in range(8)], axis=0
+    )
+
+
+def lower_inverse(gram):
+    size = gram.shape[0]
+    ids = lax.broadcasted_iota(jnp.int32, (size, 1), 0)
+    eye = (
+        lax.broadcasted_iota(jnp.int32, (size, size), 0)
+        == lax.broadcasted_iota(jnp.int32, (size, size), 1)
+    ).astype(F32)
+    aug = jnp.concatenate([gram, eye], axis=1)
+    for j in range(size):
         row = aug[j : j + 1, :]
         factor = aug[:, j : j + 1] * (1.0 / row[:, j : j + 1])
         aug = aug - jnp.where(ids > j, factor, 0.0) * row
-    return aug
+    diag = jnp.sum(aug[:, :size] * eye, axis=1, keepdims=True)
+    return aug[:, size:] * lax.rsqrt(diag)
 
 
 def exchange(
     mat_hbm, pan_hbm, out,
     mat, pan, gsend, grecv, qsend, gall, psend, precv, xsend, xrecv, piece, moved, acol, arow,
     tsend, trecv, usend, urecv,
-    ssem, rsem, msem,
+    ssem, rsem, msem, heard,
 ):
     r, c = lax.axis_index("row"), lax.axis_index("col")
     y, core, x, z = r // 2, r % 2, c // 8, c % 8
@@ -116,24 +127,22 @@
 
     pl.semaphore_wait(barrier, 27)
     put(psend.at[core_to], precv.at[core_to], 0, row_to, col_to)
+    sent(psend.at[0], 0)
 
     def scatter(i):
-        d = (r + 8 + i) % 16
-
-        @pl.when(i != 8)
-        def _():
-            put(xsend.at[d], xrecv.at[r], 3, d, c)
-
-    loop(0, 16, scatter)
+        d = (r + i) % 16
+        put(xsend.at[d], xrecv.at[r], 3, d, c)
+
+    loop(1, 16, scatter)
     keep(xsend.at[r], xrecv.at[r], 3)
+    sent(xrecv.at[pl.ds(0, 15)], 3)
     share = gsend.at[pl.ds(pl.multiple_of(8 * x, 8), 8)]
     loop(1, 16, lambda i: put(share, grecv.at[r], 2, (r + i) % 16, c))
     keep(share, grecv.at[r], 2)
-    put(psend.at[1 - core_to], precv.at[1 - core_to], 1, row_to, col_to)
-    sent(psend.at[0], 0)
-    sent(xrecv.at[pl.ds(0, 15)], 3)
     sent(grecv.at[pl.ds(0, 15)], 2)
-    sent(psend.at[0], 1)
+    loop(1, 4, lambda i: pl.semaphore_signal(
+        heard, inc=1, device_id={"row": r, "col": 8 * ((x + i) % 4) + z}, device_id_type=MESH
+    ))
     got(xrecv, 3)
     total = xrecv[0]
     for k in range(1, 16):
@@ -154,6 +163,8 @@
     loop(1, 16, share_z)
     keep(tsend, trecv.at[me], 5)
     sent(trecv.at[pl.ds(0, 15)], 5)
+    put(precv.at[core], precv.at[core], 1, r + 1 - 2 * core, c)
+    sent(precv.at[0], 1)
 
     got(grecv, 2)
     quarter = grecv[0]
@@ -164,26 +175,25 @@
     keep(qsend, gall.at[x], 8)
     sent(gall.at[pl.ds(0, 3)], 8)
 
-    loop(1, 16, lambda i: put(piece, acol.at[r], 6, (r + i) % 16, c))
-    keep(piece, acol.at[r], 6)
-    sent(acol.at[pl.ds(0, 15)], 6)
-
-    got(gall, 8)
-    packed = jnp.concatenate([gall[k] for k in range(4)], axis=0)
-    gram = jnp.concatenate([packed[:, :64], packed[:, 64:]], axis=0)
-    eye = (
-        lax.broadcasted_iota(jnp.int32, (64, 64), 0) == lax.broadcasted_iota(jnp.int32, (64, 64), 1)
-    ).astype(F32)
-    aug = jnp.concatenate([gram, eye], axis=1)
-    aug = eliminate(aug, 0, CUT1)
+    loop(1, 8, lambda i: put(piece, acol.at[core, y], 6, (r + 2 * i) % 16, c))
+    keep(piece, acol.at[core, y], 6)
+    sent(acol.at[0, pl.ds(0, 7)], 6)
 
     got(moved, 4)
-    loop(1, 32, lambda i: put(moved, arow.at[half_to, row_to], 9, r, (c + i) % 32))
+    pl.semaphore_wait(heard, 3)
+
+    def spread(i):
+        d = 8 * (i % 4) + i // 4
+
+        @pl.when(d != c)
+        def _():
+            put(moved, arow.at[half_to, row_to], 9, r, d)
+
+    loop(0, 32, spread)
     keep(moved, arow.at[half_to, row_to], 9)
     sent(arow.at[0, pl.ds(0, 15)], 9)
     sent(arow.at[1], 9)
 
-    aug = eliminate(aug, CUT1, CUT2)
     got(trecv, 5)
     total = trecv[0]
     for k in range(1, 16):
@@ -198,40 +208,48 @@
     loop(1, 32, share_xy)
     keep(usend, urecv.at[place], 7)
     sent(urecv.at[pl.ds(0, 31)], 7)
-    aug = eliminate(aug, CUT2, 64)
-    diag = jnp.sum(aug[:, :64] * eye, axis=1, keepdims=True)
-    linv = aug[:, 64:] * lax.rsqrt(diag)
+
+    got(acol.at[core], 6)
+    put(acol.at[core], acol.at[core], 10, r + 1 - 2 * core, c)
+    sent(acol.at[0], 10)
+
+    got(gall, 8)
+    packed = jnp.concatenate([gall[k] for k in range(4)], axis=0)
+    linv = lower_inverse(jnp.concatenate([packed[:, :64], packed[:, 64:]], axis=0))
 
     v_rows = dot(linv, pant)
     out[:, :1024] = v_rows
     got(precv.at[0], 1)
     v_cols = dot(linv, jnp.concatenate([precv[0], precv[1]], axis=1))
     out[:, 2048:2560] = v_cols
-    got(acol, 6)
-    av_cols = dot(linv, whole(acol, ()))
-
-    got(arow, 9)
-    even, odd = whole(arow, (0,)), whole(arow, (1,))
-    blocks = []
-    for k in range(8):
-        blocks += [even[:, 64 * k : 64 * k + 64], odd[:, 64 * k : 64 * k + 64]]
-    av_rows = dot(linv, jnp.concatenate(blocks, axis=1))
+    got(acol.at[0], 10)
+    double = 2.0 * linv
+    w_cols = dot3(double, whole(lambda y, core: acol[core, y]))
+    both = jnp.concatenate([v_rows, v_cols], axis=1)
 
     got(urecv, 7)
     rows = []
     for k in range(8):
         pair = (urecv[k] + urecv[8 + k]) + (urecv[16 + k] + urecv[24 + k])
         rows += [pair[:, :64], pair[:, 64:]]
-    corr = 2.0 * dot(dot(linv, jnp.concatenate(rows, axis=0)), linv, ((1,), (1,)))
-    out[:, 1024:2048] = 2.0 * av_rows - dot(corr, v_rows, ((0,), (0,)))
-    out[:, 2560:] = 2.0 * av_cols - dot(corr, v_cols, ((0,), (0,)))
+    corr = dot3(dot3(double, jnp.concatenate(rows, axis=0)), linv, ((1,), (1,)))
+    part = dot3(corr, both, ((0,), (0,)))
+
+    got(arow, 9)
+    even, odd = (whole(lambda y, core: arow[h, 2 * y + core]) for h in range(2))
+    blocks = []
+    for k in range(8):
+        blocks += [even[:, 64 * k : 64 * k + 64], odd[:, 64 * k : 64 * k + 64]]
+    w_rows = dot3(double, jnp.concatenate(blocks, axis=1))
+    out[:, 1024:2048] = w_rows - part[:, :1024]
+    out[:, 2560:] = w_cols - part[:, 1024:]
     finish()
 
 
 def update(mat, parts, out, w_out, v_out):
     step = pl.program_id(0)
-    first = pl.multiple_of(ROWS * step, ROWS)
-    v_rows, w_rows = parts[:, pl.ds(first, ROWS)], parts[:, pl.ds(1024 + first, ROWS)]
+    first = pl.multiple_of(512 * step, 512)
+    v_rows, w_rows = parts[:, pl.ds(first, 512)], parts[:, pl.ds(1024 + first, 512)]
     lh, ll = split(jnp.concatenate([v_rows, w_rows], axis=0).T)
     rh, rl = split(jnp.concatenate([parts[:, 2560:], parts[:, 2048:2560]], axis=0))
     out[...] = mat[...] - jnp.dot(
@@ -247,7 +265,7 @@
     parts = pl.pallas_call(
         exchange,
         out_shape=jax.ShapeDtypeStruct((64, 3072), F32),
-        in_specs=[pl.BlockSpec(memory_space=SPACE)] * 2,
+        in_specs=[pl.BlockSpec(memory_space=pltpu.HBM)] * 2,
         out_specs=vmem,
         scratch_shapes=[
             pltpu.VMEM((1024, 512), F32),
@@ -262,25 +280,26 @@
             pltpu.VMEM((16, 8, 256), F32),
             pltpu.VMEM((8, 256), F32),
             pltpu.VMEM((8, 256), F32),
-            pltpu.VMEM((16, 8, 256), F32),
+            pltpu.VMEM((2, 8, 8, 256), F32),
             pltpu.VMEM((2, 16, 8, 256), F32),
             pltpu.VMEM((4, 128), F32),
             pltpu.VMEM((16, 4, 128), F32),
             pltpu.VMEM((4, 128), F32),
             pltpu.VMEM((32, 4, 128), F32),
-            pltpu.SemaphoreType.DMA((10,)),
-            pltpu.SemaphoreType.DMA((10,)),
+            pltpu.SemaphoreType.DMA((11,)),
+            pltpu.SemaphoreType.DMA((11,)),
             pltpu.SemaphoreType.DMA((2,)),
+            pltpu.SemaphoreType.REGULAR,
         ],
         compiler_params=pltpu.CompilerParams(
-            has_side_effects=True, collective_id=0, vmem_limit_bytes=VLIM * 1024 * 1024
+            has_side_effects=True, collective_id=0, vmem_limit_bytes=52 * 1024 * 1024
         ),
     )(mat, pan.T)
-    across = pl.BlockSpec((64, ROWS), lambda i: (0, i))
-    down = pl.BlockSpec((ROWS, 512), lambda i: (i, 0))
+    across = pl.BlockSpec((64, 512), lambda i: (0, i))
+    down = pl.BlockSpec((512, 512), lambda i: (i, 0))
     updated, w_rows, v_rows = pl.pallas_call(
         update,
-        grid=(1024 // ROWS,),
+        grid=(1024 // 512,),
         out_shape=[
             jax.ShapeDtypeStruct((1024, 512), F32),
             jax.ShapeDtypeStruct((64, 1024), F32),

time: 46.4 us -> 41.1 us (0.89)
  Pallas kernels: 43.1 us -> 39.2 us
  local copies, waits for them, and re-layouts: 2.53 us -> 1.1 us
    pallas_call x1, Pallas kernels: 40.4 us -> 37.2 us  [local(): pl.pallas_call(exchange, out_shape=jax.ShapeDtypeStruct((64, 3072), F32),...]
    unnamed x4, local copies, waits for them, and re-layouts: 2.53 us -> 1.1 us
    pallas_call x1, Pallas kernels: 2.69 us -> 2.03 us  [local(): pl.pallas_call(update, grid=(1024 // 512,), out_shape=[jax.ShapeDtypeStru...]
where the time goes in v3:
time: 41.1 us; the launch traced here: 41 us
  Pallas kernels  39.2 us (95%)
  local copies, waits for them, and re-layouts  1.1 us (3%)
  between operations  0.66 us (2%)
    pallas_call x1, Pallas kernels, local(): pl.pallas_call(exchange, out_shape=jax.ShapeDtypeStruct((64, 3072), F32),...  37.2 us
    pallas_call x1, Pallas kernels, local(): pl.pallas_call(update, grid=(1024 // 512,), out_shape=[jax.ShapeDtypeStru...  2.03 us
    unnamed x4, local copies, waits for them, and re-layouts  1.1 us

profile of v3, /device:TPU:1, one launch (start us, length us, event | category | flops | bytes accessed | tf_op | source)
XLA Modules:
  0.0 41.0 jit_solution(11234016245556179248)
XLA Ops:
  0.6 0.0 copy-start
  0.6 0.0 copy-start.1
  0.6 1.1 %copy-done.1 = f32[1024,64]{0,1:T(8,128)S(1)} copy-done((f32[1024,64]{0,1:T(8,128)S(1)}, f32[1024,64]{0,1:T(8,128)}, u32[]{:S(2)}) %copy-start.1) | copy-done | bytes 262168
  1.7 37.2 %shard_map.49.parts = f32[64,3072]{1,0:T(8,128)S(1)} custom-call(f32[1024,512]{1,0:T(8,128)} %mat.1, f32[64,1024]{1,0:T(8,128)S(1)} %bitcast.3), custom_call_target="tpu_custom_call" | custom-call | tf_op jit(solution)/shard_map/pallas_call | solution.py:265
  38.9 0.0 copy-done
  38.9 2.0 %shard_map.50 = (f32[1024,512]{1,0:T(8,128)}, f32[64,1024]{1,0:T(8,128)}, f32[64,1024]{1,0:T(8,128)}) custom-call(f32[1024,512]{1,0:T(8,128)S(1)} %copy-done, f32[64,3072]{1,0:T(8,128)S(1)} %shard_map.49.parts), custom_call_target="tpu_custom_call" | custom-call | tf_op jit(solution)/shard_map/pallas_call | solution.py:300
Async XLA Ops:
  0.6 38.3 %copy-start = (f32[1024,512]{1,0:T(8,128)S(1)}, f32[1024,512]{1,0:T(8,128)}, u32[]{:S(2)}) copy-start(f32[1024,512]{1,0:T(8,128)} %mat.1) | copy-start | bytes 6291460
  0.6 1.1 %copy-start.1 = (f32[1024,64]{0,1:T(8,128)S(1)}, f32[1024,64]{0,1:T(8,128)}, u32[]{:S(2)}) copy-start(f32[1024,64]{0,1:T(8,128)} %param.3) | copy-start | bytes 786436

commit v4 on v3

--- a/solution.py
+++ b/solution.py
@@ -53,8 +53,8 @@
 
 
 def exchange(
-    mat_hbm, pan_hbm, out,
-    mat, pan, gsend, grecv, qsend, gall, psend, precv, xsend, xrecv, piece, moved, acol, arow,
+    mat_hbm, pan_hbm, mat, out,
+    pan, gsend, grecv, qsend, gall, psend, precv, xsend, xrecv, piece, moved, acol, arow,
     tsend, trecv, usend, urecv,
     ssem, rsem, msem, heard,
 ):
@@ -227,6 +227,13 @@
     w_cols = dot3(double, whole(lambda y, core: acol[core, y]))
     both = jnp.concatenate([v_rows, v_cols], axis=1)
 
+    got(arow, 9)
+    even, odd = (whole(lambda y, core: arow[h, 2 * y + core]) for h in range(2))
+    blocks = []
+    for k in range(8):
+        blocks += [even[:, 64 * k : 64 * k + 64], odd[:, 64 * k : 64 * k + 64]]
+    w_rows = dot3(double, jnp.concatenate(blocks, axis=1))
+
     got(urecv, 7)
     rows = []
     for k in range(8):
@@ -234,41 +241,45 @@
         rows += [pair[:, :64], pair[:, 64:]]
     corr = dot3(dot3(double, jnp.concatenate(rows, axis=0)), linv, ((1,), (1,)))
     part = dot3(corr, both, ((0,), (0,)))
-
-    got(arow, 9)
-    even, odd = (whole(lambda y, core: arow[h, 2 * y + core]) for h in range(2))
-    blocks = []
-    for k in range(8):
-        blocks += [even[:, 64 * k : 64 * k + 64], odd[:, 64 * k : 64 * k + 64]]
-    w_rows = dot3(double, jnp.concatenate(blocks, axis=1))
     out[:, 1024:2048] = w_rows - part[:, :1024]
     out[:, 2560:] = w_cols - part[:, 1024:]
     finish()
 
 
-def update(mat, parts, out, w_out, v_out):
-    step = pl.program_id(0)
-    first = pl.multiple_of(512 * step, 512)
-    v_rows, w_rows = parts[:, pl.ds(first, 512)], parts[:, pl.ds(1024 + first, 512)]
-    lh, ll = split(jnp.concatenate([v_rows, w_rows], axis=0).T)
+def update(mat, parts, out_hbm, w_hbm, v_hbm, out, sems):
+    thin = [
+        pltpu.make_async_copy(parts.at[:, pl.ds(1024, 1024)], w_hbm, sems.at[0]),
+        pltpu.make_async_copy(parts.at[:, pl.ds(0, 1024)], v_hbm, sems.at[1]),
+    ]
+    for copy in thin:
+        copy.start()
     rh, rl = split(jnp.concatenate([parts[:, 2560:], parts[:, 2048:2560]], axis=0))
-    out[...] = mat[...] - jnp.dot(
-        jnp.concatenate([lh, lh, ll], axis=1), jnp.concatenate([rh, rl, rh], axis=0),
-        preferred_element_type=F32,
-    )
-    w_out[...] = w_rows
-    v_out[...] = v_rows
+    right = jnp.concatenate([rh, rl, rh], axis=0)
+    copies = []
+    for k in range(0, 1024, 256):
+        rows = pl.ds(k, 256)
+        left = jnp.concatenate([parts[:, k : k + 256], parts[:, 1024 + k : 1024 + k + 256]], axis=0).T
+        lh, ll = split(left)
+        out[rows, :] = mat[rows, :] - jnp.dot(
+            jnp.concatenate([lh, lh, ll], axis=1), right, preferred_element_type=F32
+        )
+        copies.append(pltpu.make_async_copy(out.at[rows], out_hbm.at[rows], sems.at[2 + k // 256]))
+        copies[-1].start()
+    for copy in thin + copies:
+        copy.wait()
 
 
 def local(mat, pan):
     vmem = pl.BlockSpec(memory_space=pltpu.VMEM)
-    parts = pl.pallas_call(
+    held, parts = pl.pallas_call(
         exchange,
-        out_shape=jax.ShapeDtypeStruct((64, 3072), F32),
+        out_shape=[
+            jax.ShapeDtypeStruct((1024, 512), F32),
+            jax.ShapeDtypeStruct((64, 3072), F32),
+        ],
         in_specs=[pl.BlockSpec(memory_space=pltpu.HBM)] * 2,
-        out_specs=vmem,
+        out_specs=[vmem] * 2,
         scratch_shapes=[
-            pltpu.VMEM((1024, 512), F32),
             pltpu.VMEM((64, 1024), F32),
             pltpu.VMEM((32, 128), F32),
             pltpu.VMEM((16, 8, 128), F32),
@@ -292,23 +303,21 @@
             pltpu.SemaphoreType.REGULAR,
         ],
         compiler_params=pltpu.CompilerParams(
-            has_side_effects=True, collective_id=0, vmem_limit_bytes=52 * 1024 * 1024
+            has_side_effects=True, collective_id=0, vmem_limit_bytes=50 * 1024 * 1024
         ),
     )(mat, pan.T)
-    across = pl.BlockSpec((64, 512), lambda i: (0, i))
-    down = pl.BlockSpec((512, 512), lambda i: (i, 0))
     updated, w_rows, v_rows = pl.pallas_call(
         update,
-        grid=(1024 // 512,),
         out_shape=[
             jax.ShapeDtypeStruct((1024, 512), F32),
             jax.ShapeDtypeStruct((64, 1024), F32),
             jax.ShapeDtypeStruct((64, 1024), F32),
         ],
-        in_specs=[down, pl.BlockSpec((64, 3072), lambda i: (0, 0))],
-        out_specs=[down, across, across],
+        in_specs=[vmem] * 2,
+        out_specs=[pl.BlockSpec(memory_space=pltpu.HBM)] * 3,
+        scratch_shapes=[pltpu.VMEM((1024, 512), F32), pltpu.SemaphoreType.DMA((2 + 1024 // 256,))],
         compiler_params=pltpu.CompilerParams(vmem_limit_bytes=32 * 1024 * 1024),
-    )(mat, parts)
+    )(held, parts)
     return updated, w_rows.T, v_rows.T
 
 

time: 41.1 us -> 40.3 us (0.981)
  Pallas kernels: 39.2 us -> 38.6 us
    pallas_call x2, Pallas kernels: 39.2 us -> 38.6 us  [the longest x1 36.9 us: local(): pl.pallas_call(exchange, out_shape=[jax.ShapeDtypeStruct((1024, 512), F32...]
    unnamed x4 -> x2, local copies, waits for them, and re-layouts: 1.1 us -> 0.94 us
where the time goes in v4:
time: 40.3 us; the launch traced here: 40.2 us
  Pallas kernels  38.6 us (96%)
  local copies, waits for them, and re-layouts  0.94 us (2%)
  between operations  0.65 us (2%)
    pallas_call x1, Pallas kernels, local(): pl.pallas_call(exchange, out_shape=[jax.ShapeDtypeStruct((1024, 512), F32...  36.9 us
    pallas_call x1, Pallas kernels, local(): pl.pallas_call(update, out_shape=[jax.ShapeDtypeStruct((1024, 512), F32),...  1.7 us
    unnamed x2, local copies, waits for them, and re-layouts  0.94 us

profile of v4, /device:TPU:1, one launch (start us, length us, event | category | flops | bytes accessed | tf_op | source)
XLA Modules:
  0.0 40.2 jit_solution(11880106926154425141)
XLA Ops:
  0.6 0.0 copy-start
  0.6 0.9 %copy-done = f32[1024,64]{0,1:T(8,128)S(1)} copy-done((f32[1024,64]{0,1:T(8,128)S(1)}, f32[1024,64]{0,1:T(8,128)}, u32[]{:S(2)}) %copy-start) | copy-done | bytes 262168
  1.6 36.9 %shard_map.49 = (f32[1024,512]{1,0:T(8,128)S(1)}, f32[64,3072]{1,0:T(8,128)S(1)}) custom-call(f32[1024,512]{1,0:T(8,128)} %mat_hbm.1, f32[64,1024]{1,0:T(8,128)S(1)} %bitcast.3), custom_call_target="tpu_custom_call" | custom-call | tf_op jit(solution)/shard_map/pallas_call | solution.py:274
  38.5 1.7 %shard_map.50 = (f32[1024,512]{1,0:T(8,128)}, f32[64,1024]{1,0:T(8,128)}, f32[64,1024]{1,0:T(8,128)}) custom-call(f32[1024,512]{1,0:T(8,128)S(1)} %get-tuple-element.8.mat, f32[64,3072]{1,0:T(8,128)S(1)} %get-tuple-element.9.parts), custom_call_target="tpu_custom_call" | custom-call | tf_op jit(solution)/shard_map/pallas_call | solution.py:309
Async XLA Ops:
  0.6 1.0 %copy-start = (f32[1024,64]{0,1:T(8,128)S(1)}, f32[1024,64]{0,1:T(8,128)}, u32[]{:S(2)}) copy-start(f32[1024,64]{0,1:T(8,128)} %param.3) | copy-start | bytes 786436

commit v5 on v4

--- a/solution.py
+++ b/solution.py
@@ -53,8 +53,8 @@
 
 
 def exchange(
-    mat_hbm, pan_hbm, mat, out,
-    pan, gsend, grecv, qsend, gall, psend, precv, xsend, xrecv, piece, moved, acol, arow,
+    mat_hbm, pan, mat, out,
+    gsend, grecv, qsend, gall, psend, precv, xsend, xrecv, piece, moved, acol, arow,
     tsend, trecv, usend, urecv,
     ssem, rsem, msem, heard,
 ):
@@ -91,8 +91,6 @@
 
     load = pltpu.make_async_copy(mat_hbm, mat, msem.at[0])
     load.start()
-    load_pan = pltpu.make_async_copy(pan_hbm, pan, msem.at[1])
-    load_pan.start()
 
     core_to = (x - r // 8) % 2
     x_to = (x - core_to) % 4
@@ -106,7 +104,6 @@
     loop(1, 8, lambda i: greet(r, 8 * x + (z + i) % 8))
     loop(1, 4, lambda i: greet(r, 8 * ((x + i) % 4) + z))
 
-    load_pan.wait()
     for k in range(4):
         low, high = pan[:, 256 * k : 256 * k + 128], pan[:, 256 * k + 128 : 256 * k + 256]
         psend[k // 2, :, 128 * (k % 2) : 128 * (k % 2) + 128] = jnp.where(
@@ -126,8 +123,10 @@
         xsend[k] = prod[8 * (k // 2) : 8 * (k // 2) + 8, 256 * (k % 2) : 256 * (k % 2) + 256]
 
     pl.semaphore_wait(barrier, 27)
-    put(psend.at[core_to], precv.at[core_to], 0, row_to, col_to)
-    sent(psend.at[0], 0)
+    put(psend.at[core_to, pl.ds(0, 32)], precv.at[core_to, pl.ds(0, 32)], 0, row_to, col_to)
+    put(psend.at[core_to, pl.ds(32, 32)], precv.at[core_to, pl.ds(32, 32)], 11, row_to, col_to)
+    sent(psend.at[0, pl.ds(0, 32)], 0)
+    sent(psend.at[0, pl.ds(0, 32)], 11)
 
     def scatter(i):
         d = (r + i) % 16
@@ -151,8 +150,9 @@
     put(piece, moved, 4, row_up, col_up)
     sent(piece, 4)
 
-    got(precv.at[core], 0)
-    tpart = dot(total, precv[core], ((1,), (1,)))
+    got(precv.at[core, pl.ds(0, 32)], 0)
+    got(precv.at[core, pl.ds(0, 32)], 11)
+    tpart = dot3(total, precv[core], ((1,), (1,)))
     tsend[...] = jnp.concatenate([tpart[:4], tpart[4:]], axis=1)
     me = 2 * z + core
 
@@ -227,6 +227,7 @@
     w_cols = dot3(double, whole(lambda y, core: acol[core, y]))
     both = jnp.concatenate([v_rows, v_cols], axis=1)
 
+    finish()
     got(arow, 9)
     even, odd = (whole(lambda y, core: arow[h, 2 * y + core]) for h in range(2))
     blocks = []
@@ -243,7 +244,6 @@
     part = dot3(corr, both, ((0,), (0,)))
     out[:, 1024:2048] = w_rows - part[:, :1024]
     out[:, 2560:] = w_cols - part[:, 1024:]
-    finish()
 
 
 def update(mat, parts, out_hbm, w_hbm, v_hbm, out, sems):
@@ -277,10 +277,9 @@
             jax.ShapeDtypeStruct((1024, 512), F32),
             jax.ShapeDtypeStruct((64, 3072), F32),
         ],
-        in_specs=[pl.BlockSpec(memory_space=pltpu.HBM)] * 2,
+        in_specs=[pl.BlockSpec(memory_space=pltpu.HBM), vmem],
         out_specs=[vmem] * 2,
         scratch_shapes=[
-            pltpu.VMEM((64, 1024), F32),
             pltpu.VMEM((32, 128), F32),
             pltpu.VMEM((16, 8, 128), F32),
             pltpu.VMEM((8, 128), F32),
@@ -297,8 +296,8 @@
             pltpu.VMEM((16, 4, 128), F32),
             pltpu.VMEM((4, 128), F32),
             pltpu.VMEM((32, 4, 128), F32),
-            pltpu.SemaphoreType.DMA((11,)),
-            pltpu.SemaphoreType.DMA((11,)),
+            pltpu.SemaphoreType.DMA((12,)),
+            pltpu.SemaphoreType.DMA((12,)),
             pltpu.SemaphoreType.DMA((2,)),
             pltpu.SemaphoreType.REGULAR,
         ],

time: 40.3 us -> 40.2 us (level)
  no operation moved by 1% of the time
where the time goes in v5:
time: 40.2 us; the launch traced here: 40 us
  Pallas kernels  38.5 us (96%)
  local copies, waits for them, and re-layouts  0.94 us (2%)
  between operations  0.65 us (2%)
    pallas_call x1, Pallas kernels, local(): pl.pallas_call(exchange, out_shape=[jax.ShapeDtypeStruct((1024, 512), F32...  36.7 us
    pallas_call x1, Pallas kernels, local(): pl.pallas_call(update, out_shape=[jax.ShapeDtypeStruct((1024, 512), F32),...  1.7 us
    unnamed x2, local copies, waits for them, and re-layouts  0.94 us

profile of v5, /device:TPU:1, one launch (start us, length us, event | category | flops | bytes accessed | tf_op | source)
XLA Modules:
  0.0 40.0 jit_solution(13853179000974289627)
XLA Ops:
  0.6 0.0 copy-start
  0.6 0.9 %copy-done = f32[1024,64]{0,1:T(8,128)S(1)} copy-done((f32[1024,64]{0,1:T(8,128)S(1)}, f32[1024,64]{0,1:T(8,128)}, u32[]{:S(2)}) %copy-start) | copy-done | bytes 262168
  1.6 36.7 %shard_map.49 = (f32[1024,512]{1,0:T(8,128)S(1)}, f32[64,3072]{1,0:T(8,128)S(1)}) custom-call(f32[1024,512]{1,0:T(8,128)} %mat_hbm.1, f32[64,1024]{1,0:T(8,128)S(1)} %bitcast.3), custom_call_target="tpu_custom_call" | custom-call | tf_op jit(solution)/shard_map/pallas_call | solution.py:274
  38.3 1.7 %shard_map.50 = (f32[1024,512]{1,0:T(8,128)}, f32[64,1024]{1,0:T(8,128)}, f32[64,1024]{1,0:T(8,128)}) custom-call(f32[1024,512]{1,0:T(8,128)S(1)} %get-tuple-element.8.mat, f32[64,3072]{1,0:T(8,128)S(1)} %get-tuple-element.9.parts), custom_call_target="tpu_custom_call" | custom-call | tf_op jit(solution)/shard_map/pallas_call | solution.py:308
Async XLA Ops:
  0.6 1.0 %copy-start = (f32[1024,64]{0,1:T(8,128)S(1)}, f32[1024,64]{0,1:T(8,128)}, u32[]{:S(2)}) copy-start(f32[1024,64]{0,1:T(8,128)} %param.3) | copy-start | bytes 786436
